TPU v7x, 512 devices: a whole 4x8x8 slice. The times are simulated.
512 devices in a mesh: lon: 32 (over z_lo, x, core), lat: 16 (over y, z_hi).
Axes of the slice: x: 4, y: 8, z: 8 (z_hi: 2, z_lo: 4; z = z_hi * 4 + z_lo), core: 2. Of those that a mesh axis runs over, the one named last changes fastest.
Arguments:
- fields: bfloat16 [768, 1536, 128], P('lat', 'lon'), may hold values from -6 to 6
- cotangent: bfloat16 [768, 1536, 128], P('lat', 'lon'), may hold values from -6 to 6
- mixing: bfloat16 [9, 128, 128], replicated, may hold values from -0.1875 to 0.1875
- widths: int32 [768, 5], replicated, may hold values from 1 to 16, as said below
Outputs:
- features_out: bfloat16 [768, 1536, 128], P('lat', 'lon')
- grad_input: bfloat16 [768, 1536, 128], P('lat', 'lon')
Inputs may be any that keep to these rules, and one draw needn't show every extreme that they name: `widths`: rows 0 and 767 have 16 at every row offset.
All inputs are finite; a program needn't handle non-finite values.
Results may differ from a plain program's by a relative error of at most 0.006.
Values may be sent and summed in bfloat16 or wider, within the bound.
A program may use at most 64 MiB of HBM per device.

v0:
```python
import functools

import jax
import jax.numpy as jnp
from jax import lax
from jax.experimental import pallas as pl
from jax.experimental.pallas import tpu as pltpu
from jax.sharding import PartitionSpec as P

RAD = 2
HALO = 16
SPAN = 2 * RAD + 1
BLOCK = 16
REACH = BLOCK + 2 * HALO
TAPS = 256
CENTERS = (-0.5, 0.0, 0.5)


def padded_2(cells, sides, width, closed):
    for axis, dim in sides:
        count = lax.axis_size(axis)
        ends = count if closed else count - 1
        head = lax.slice_in_dim(cells, 0, width, axis=dim)
        tail = lax.slice_in_dim(cells, cells.shape[dim] - width, cells.shape[dim], axis=dim)
        cells = jnp.concatenate(
            [
                lax.ppermute(tail, axis, [(i, (i + 1) % count) for i in range(ends)]),
                cells,
                lax.ppermute(head, axis, [((i + 1) % count, i) for i in range(ends)]),
            ],
            axis=dim,
        )
    return cells


def widths_by_tap(widths, local, wide):
    rows = wide.shape[1]
    total = widths.shape[0]
    first = lax.axis_index("lat") * rows
    start = jnp.clip(first - 8, 0, total - rows - 16)
    start = pl.multiple_of(start, 8)
    local[...] = jnp.zeros_like(local)
    local[pl.ds(pl.multiple_of(start - first + 16, 8), rows + 16), :] = widths[
        pl.ds(start, rows + 16), :
    ].astype(jnp.float32)
    source = lax.broadcasted_iota(jnp.int32, (SPAN, TAPS), 0)
    tap_row = lax.broadcasted_iota(jnp.int32, (SPAN, TAPS), 1) // REACH
    own = (source == tap_row).astype(jnp.bfloat16)
    dot = functools.partial(jnp.dot, preferred_element_type=jnp.float32)
    wide[0] = dot(local[16 : 16 + rows, :].astype(jnp.bfloat16), own)
    turned = jnp.zeros((rows, TAPS), jnp.float32)
    for r in range(SPAN):
        pick = ((source == SPAN - 1 - r) & (tap_row == r)).astype(jnp.bfloat16)
        turned += dot(local[16 + r - RAD : 16 + r - RAD + rows, :].astype(jnp.bfloat16), pick)
    wide[1] = turned


def taps(foot_width):
    lane = lax.broadcasted_iota(jnp.int32, (BLOCK, TAPS), 1)
    tap_row = lane // REACH
    offset = (
        lane - tap_row * REACH - lax.broadcasted_iota(jnp.int32, (BLOCK, TAPS), 0) - HALO
    ).astype(jnp.float32)
    across = (tap_row[:1].astype(jnp.float32) - RAD) / (RAD + 1.0)
    norm = 3.0 / (2.0 * foot_width + 1.0)
    inside = jnp.abs(offset) <= foot_width
    along = offset * (1.0 / (foot_width + 1.0))
    pieces = []
    scales = [norm * jnp.maximum(0.0, 1.0 - 2.0 * jnp.abs(across - c)) for c in CENTERS]
    for lon_center in CENTERS:
        hat = jnp.maximum(0.0, 1.0 - 2.0 * jnp.abs(along - lon_center))
        hat = jnp.where(inside, hat, 0.0)
        pieces += [(hat * scale).astype(jnp.bfloat16) for scale in scales]
    return jnp.concatenate(pieces, axis=0)


def kernel(cells, mixing, widths, features, gradient, local, wide, basis, turned):
    rows, columns, channels = features.shape
    count = mixing.shape[0]
    blocks = columns // BLOCK
    group = basis.shape[0] // columns
    widths_by_tap(widths, local, wide)
    for k in range(count):
        turned[0, k * channels : (k + 1) * channels, :] = mixing[k]
        turned[1, k * channels : (k + 1) * channels, :] = (
            mixing[count - 1 - k].astype(jnp.float32).T.astype(jnp.bfloat16)
        )
    for side, result in enumerate((features, gradient)):

        def rows_of(step, carry, side=side, result=result):
            def one_row(slot, carry):
                row = step * group + slot
                coeffs = taps(wide[side, pl.ds(row, 1), :])
                data = jnp.concatenate(
                    [
                        jnp.concatenate(
                            [
                                cells[side, row + r, BLOCK * b : BLOCK * b + REACH, :]
                                for r in range(SPAN)
                            ]
                            + [cells[side, row, :TAPS - SPAN * REACH, :]],
                            axis=0,
                        )
                        for b in range(blocks)
                    ],
                    axis=1,
                )
                out = jnp.dot(coeffs, data, preferred_element_type=jnp.float32).astype(jnp.bfloat16)
                for b in range(blocks):
                    for k in range(count):
                        basis[
                            pl.ds(pl.multiple_of(slot * columns + BLOCK * b, BLOCK), BLOCK),
                            k * channels : (k + 1) * channels,
                        ] = out[k * BLOCK : (k + 1) * BLOCK, b * channels : (b + 1) * channels]
                return carry

            lax.fori_loop(0, group, one_row, 0)
            mixed = jnp.dot(basis[...], turned[side], preferred_element_type=jnp.float32)
            result[pl.ds(step * group, group)] = mixed.astype(jnp.bfloat16).reshape(
                group, columns, channels
            )
            return carry

        lax.fori_loop(0, rows // group, rows_of, 0)


def body(fields, cotangent, mixing, widths):
    rows, columns, channels = fields.shape
    count = mixing.shape[0]
    group = 8
    cells = jnp.stack([fields, cotangent])
    cells = padded_2(cells, (("lat", 1),), RAD, False)
    cells = padded_2(cells, (("lon", 2),), HALO, True)
    shape = jax.ShapeDtypeStruct(fields.shape, jnp.bfloat16)
    vmem = pl.BlockSpec(memory_space=pltpu.VMEM)
    return pl.pallas_call(
        kernel,
        out_shape=(shape, shape),
        in_specs=[vmem] * 3,
        out_specs=(vmem, vmem),
        scratch_shapes=[
            pltpu.VMEM((rows + 32, SPAN), jnp.float32),
            pltpu.VMEM((2, rows, TAPS), jnp.float32),
            pltpu.VMEM((group * columns, count * channels), jnp.bfloat16),
            pltpu.VMEM((2, count * channels, channels), jnp.bfloat16),
        ],
        compiler_params=pltpu.CompilerParams(vmem_limit_bytes=48 * 1024 * 1024),
    )(cells, mixing, widths)


def solution(mesh):
    in_specs = (P("lat", "lon", None), P("lat", "lon", None), P(), P())
    out_specs = (P("lat", "lon", None), P("lat", "lon", None))
    return jax.shard_map(body, mesh=mesh, in_specs=in_specs, out_specs=out_specs, check_vma=False)
```

profile of v0, /device:TPU:1, one launch (start us, length us, event | category | flops | bytes accessed | tf_op | source)
XLA Modules:
  0.0 65.1 jit_solution(11490894940872540269)
XLA Ops:
  0.6 0.0 copy-start.1
  0.6 0.0 copy-start.2
  0.7 0.0 copy-start.3
  0.7 0.9 %pad_maximum_fusion.6 = (bf16[2,2,48,128]{3,2,1,0:T(8,128)(2,1)S(1)}, bf16[2,2,48,128]{3,2,1,0:T(8,128)(2,1)S(1)}) fusion(bf16[1,48,48,128]{3,2,1,0:T(8,128)(2,1)} %bitcast.2, bf16[1,48,48,128]{3,2,1,0:T(8,128)(2,1)} %bitcast.5), kind=kLoop, calls=%fused_computation.6 | loop fusion | flops 49152 | bytes 1277952 | tf_op jit(solution)/shard_map/slice | solution.py:24
  1.6 11.5 %collective-permute-start = (bf16[2,2,48,128]{3,2,1,0:T(8,128)(2,1)S(1)}, bf16[2,2,48,128]{3,2,1,0:T(8,128)(2,1)S(1)}, u32[]{:S(2)}, u32[]{:S(2)}) collective-permute-start(bf16[2,2,48,128]{3,2,1,0:T(8,128)(2,1)S(1)} %get-tuple-element.4), channel_id=1, source_target_pairs={{0,1},{1,2},{2,3},{3,4},{4,5},{5,6},{6,7},{7,8},{8,9},{9,10},{10,1... | collective-permute-start | bytes 147464 | tf_op jit(solution)/shard_map/ppermute | solution.py:27
  13.0 1.3 %collective-permute-start.1 = (bf16[2,2,48,128]{3,2,1,0:T(8,128)(2,1)S(1)}, bf16[2,2,48,128]{3,2,1,0:T(8,128)(2,1)S(1)}, u32[]{:S(2)}, u32[]{:S(2)}) collective-permute-start(bf16[2,2,48,128]{3,2,1,0:T(8,128)(2,1)S(1)} %get-tuple-element.5), channel_id=1, source_target_pairs={{1,0},{2,1},{3,2},{4,3},{5,4},{6,5},{7,6},{8,7},{9,8},{10,9},{11,1... | collective-permute-start | bytes 147464 | tf_op jit(solution)/shard_map/ppermute | solution.py:29
  14.3 0.0 collective-permute-done
  14.3 7.5 %collective-permute-done.1 = bf16[2,2,48,128]{3,2,1,0:T(8,128)(2,1)S(1)} collective-permute-done((bf16[2,2,48,128]{3,2,1,0:T(8,128)(2,1)S(1)}, bf16[2,2,48,128]{3,2,1,0:T(8,128)(2,1)S(1)}, u32[]{:S(2)}, u32[]{:S(2)}) %collective-permute-start.1) | collective-permute-done | bytes 49184 | tf_op jit(solution)/shard_map/ppermute | solution.py:29
  21.8 1.4 %pad_maximum_fusion.4 = (bf16[2,52,16,128]{3,2,1,0:T(8,128)(2,1)S(1)}, bf16[2,52,16,128]{3,2,1,0:T(8,128)(2,1)S(1)}) fusion(bf16[2,2,48,128]{3,2,1,0:T(8,128)(2,1)S(1)} %collective-permute-done.1, bf16[2,2,48,128]{3,2,1,0:T(8,128)(2,1)S(1)} %collective-permute-done, bf16[1,48,48,128]{3,2,1,0:T(8,128)(2,1)} %bitcast.3, bf16[1,48,48,128]{3,2,1,0:T(8,128)(2,1)} %bitcast.6), kind=kLoop, calls=%fused_computation.4 | loop fusion | flops 3407872 | bytes 2129920 | tf_op jit(solution)/shard_map/slice | solution.py:24
  23.2 5.5 %collective-permute-start.2 = (bf16[2,52,16,128]{3,2,1,0:T(8,128)(2,1)S(1)}, bf16[2,52,16,128]{3,2,1,0:T(8,128)(2,1)S(1)}, u32[]{:S(2)}, u32[]{:S(2)}) collective-permute-start(bf16[2,52,16,128]{3,2,1,0:T(8,128)(2,1)S(1)} %get-tuple-element.2), channel_id=1, source_target_pairs={{0,16},{16,32},{32,48},{48,64},{64,80},{80,96},{96,112},{112,128},... | collective-permute-start | bytes 1277960 | tf_op jit(solution)/shard_map/ppermute | solution.py:27
  28.7 1.9 %collective-permute-start.3 = (bf16[2,52,16,128]{3,2,1,0:T(8,128)(2,1)S(1)}, bf16[2,52,16,128]{3,2,1,0:T(8,128)(2,1)S(1)}, u32[]{:S(2)}, u32[]{:S(2)}) collective-permute-start(bf16[2,52,16,128]{3,2,1,0:T(8,128)(2,1)S(1)} %get-tuple-element.3), channel_id=1, source_target_pairs={{16,0},{32,16},{48,32},{64,48},{80,64},{96,80},{112,96},{128,112},... | collective-permute-start | bytes 1277960 | tf_op jit(solution)/shard_map/ppermute | solution.py:29
  30.6 0.0 copy-done.3
  30.7 0.2 copy.6.widths
  30.8 0.0 copy-start
  30.9 2.9 %collective-permute-done.2 = bf16[2,52,16,128]{3,2,1,0:T(8,128)(2,1)S(1)} collective-permute-done((bf16[2,52,16,128]{3,2,1,0:T(8,128)(2,1)S(1)}, bf16[2,52,16,128]{3,2,1,0:T(8,128)(2,1)S(1)}, u32[]{:S(2)}, u32[]{:S(2)}) %collective-permute-start.2) | collective-permute-done | bytes 426016 | tf_op jit(solution)/shard_map/ppermute | solution.py:27
  33.8 4.7 %collective-permute-done.3 = bf16[2,52,16,128]{3,2,1,0:T(8,128)(2,1)S(1)} collective-permute-done((bf16[2,52,16,128]{3,2,1,0:T(8,128)(2,1)S(1)}, bf16[2,52,16,128]{3,2,1,0:T(8,128)(2,1)S(1)}, u32[]{:S(2)}, u32[]{:S(2)}) %collective-permute-start.3) | collective-permute-done | bytes 426016 | tf_op jit(solution)/shard_map/ppermute | solution.py:29
  38.5 0.0 copy-done.1
  38.5 0.0 copy-done.2
  38.5 1.2 %pad_maximum_fusion.cells = bf16[2,52,80,128]{3,2,1,0:T(8,128)(2,1)S(1)} fusion(bf16[2,52,16,128]{3,2,1,0:T(8,128)(2,1)S(1)} %collective-permute-done.3, bf16[2,2,48,128]{3,2,1,0:T(8,128)(2,1)S(1)} %collective-permute-done.1, bf16[1,48,48,128]{3,2,1,0:T(8,128)(2,1)S(1)} %bitcast.4, bf16[1,48,48,128]{3,2,1,0:T(8,128)(2,1)S(1)} %bitcast.7, ...), kind=kLoop, calls=%fused_computation | loop fusion | flops 12779520 | bytes 4259840 | tf_op jit(solution)/shard_map/concatenate | solution.py:25
  39.6 0.0 copy-done
  39.7 25.5 %shard_map.59 = (bf16[48,48,128]{2,1,0:T(8,128)(2,1)}, bf16[48,48,128]{2,1,0:T(8,128)(2,1)}) custom-call(bf16[2,52,80,128]{3,2,1,0:T(8,128)(2,1)S(1)} %pad_maximum_fusion.cells, bf16[9,128,128]{2,1,0:T(8,128)(2,1)S(1)} %copy-done, s32[768,5]{1,0:T(8,128)S(1)} %copy.6.widths), custom_call_target="tpu_custom_call" | custom-call | tf_op jit(solution)/shard_map/pallas_call | solution.py:136
Async XLA Ops:
  0.6 37.8 %copy-start.1 = (bf16[48,48,128]{2,1,0:T(8,128)(2,1)S(1)}, bf16[48,48,128]{2,1,0:T(8,128)(2,1)}, u32[]{:S(2)}) copy-start(bf16[48,48,128]{2,1,0:T(8,128)(2,1)} %param.5) | copy-start | bytes 1769476
  0.6 37.8 %copy-start.2 = (bf16[48,48,128]{2,1,0:T(8,128)(2,1)S(1)}, bf16[48,48,128]{2,1,0:T(8,128)(2,1)}, u32[]{:S(2)}) copy-start(bf16[48,48,128]{2,1,0:T(8,128)(2,1)} %param.4) | copy-start | bytes 1769476
  0.7 30.0 %copy-start.3 = (s32[768,5]{0,1:T(8,128)S(1)}, s32[768,5]{0,1:T(8,128)}, u32[]{:S(2)}) copy-start(s32[768,5]{0,1:T(8,128)} %param.7) | copy-start | bytes 46084
  1.6 12.8 %collective-permute-start = (bf16[2,2,48,128]{3,2,1,0:T(8,128)(2,1)S(1)}, bf16[2,2,48,128]{3,2,1,0:T(8,128)(2,1)S(1)}, u32[]{:S(2)}, u32[]{:S(2)}) collective-permute-start(bf16[2,2,48,128]{3,2,1,0:T(8,128)(2,1)S(1)} %get-tuple-element.4), channel_id=1, source_target_pairs={{0,1},{1,2},{2,3},{3,4},{4,5},{5,6},{6,7},{7,8},{8,9},{9,10},{10,1... | collective-permute-start | bytes 147464 | tf_op jit(solution)/shard_map/ppermute | solution.py:27
  13.0 8.8 %collective-permute-start.1 = (bf16[2,2,48,128]{3,2,1,0:T(8,128)(2,1)S(1)}, bf16[2,2,48,128]{3,2,1,0:T(8,128)(2,1)S(1)}, u32[]{:S(2)}, u32[]{:S(2)}) collective-permute-start(bf16[2,2,48,128]{3,2,1,0:T(8,128)(2,1)S(1)} %get-tuple-element.5), channel_id=1, source_target_pairs={{1,0},{2,1},{3,2},{4,3},{5,4},{6,5},{7,6},{8,7},{9,8},{10,9},{11,1... | collective-permute-start | bytes 147464 | tf_op jit(solution)/shard_map/ppermute | solution.py:29
  23.2 10.6 %collective-permute-start.2 = (bf16[2,52,16,128]{3,2,1,0:T(8,128)(2,1)S(1)}, bf16[2,52,16,128]{3,2,1,0:T(8,128)(2,1)S(1)}, u32[]{:S(2)}, u32[]{:S(2)}) collective-permute-start(bf16[2,52,16,128]{3,2,1,0:T(8,128)(2,1)S(1)} %get-tuple-element.2), channel_id=1, source_target_pairs={{0,16},{16,32},{32,48},{48,64},{64,80},{80,96},{96,112},{112,128},... | collective-permute-start | bytes 1277960 | tf_op jit(solution)/shard_map/ppermute | solution.py:27
  28.7 9.7 %collective-permute-start.3 = (bf16[2,52,16,128]{3,2,1,0:T(8,128)(2,1)S(1)}, bf16[2,52,16,128]{3,2,1,0:T(8,128)(2,1)S(1)}, u32[]{:S(2)}, u32[]{:S(2)}) collective-permute-start(bf16[2,52,16,128]{3,2,1,0:T(8,128)(2,1)S(1)} %get-tuple-element.3), channel_id=1, source_target_pairs={{16,0},{32,16},{48,32},{64,48},{80,64},{96,80},{112,96},{128,112},... | collective-permute-start | bytes 1277960 | tf_op jit(solution)/shard_map/ppermute | solution.py:29
  30.8 8.8 %copy-start = (bf16[9,128,128]{2,1,0:T(8,128)(2,1)S(1)}, bf16[9,128,128]{2,1,0:T(8,128)(2,1)}, u32[]{:S(2)}) copy-start(bf16[9,128,128]{2,1,0:T(8,128)(2,1)} %mixing.1) | copy-start | bytes 884740
where the time goes:
time: 66.3 us; the launch traced here: 65.1 us
  Pallas kernels  25.5 us (38%)
  starting transfers between devices  20.2 us (30%)
  waiting for transfers between devices  15.1 us (23%)
  other arithmetic  3.44 us (5%)
  between operations  0.74 us (1%)
    pallas_call x1, Pallas kernels, body(): pl.pallas_call(kernel, out_shape=(shape, shape), in_specs=[vmem] * 3, out...  25.5 us
    ppermute x2, starting transfers between devices, padded_2(): lax.ppermute(tail, axis, [(i, (i + 1) % count) for i in range(ends)])  17 us
    ppermute x2, waiting for transfers between devices, padded_2(): lax.ppermute(head, axis, [((i + 1) % count, i) for i in range(ends)])  12.2 us
    ppermute x2, starting transfers between devices, padded_2(): lax.ppermute(head, axis, [((i + 1) % count, i) for i in range(ends)])  3.21 us
    ppermute x2, waiting for transfers between devices, padded_2(): lax.ppermute(tail, axis, [(i, (i + 1) % count) for i in range(ends)])  2.91 us
    slice x2, other arithmetic, padded_2(): lax.slice_in_dim(cells, cells.shape[dim] - width, cells.shape[dim], axis=...  2.28 us
  transfers between devices with their start and end apart: 4, of which 3 were waited for; matrix products, arithmetic and copies ran while one was open for 0% of the time, Pallas kernels for 0%

commit v1 on v0

v1 whole, which is shorter than its diff:
```python
import functools

import jax
import jax.numpy as jnp
from jax import lax
from jax.experimental import pallas as pl
from jax.experimental.pallas import tpu as pltpu
from jax.sharding import PartitionSpec as P

RAD = 2
HALO = 16
SPAN = 2 * RAD + 1
BLOCK = 16
REACH = BLOCK + 2 * HALO
TAPS = 256
CENTERS = (-0.5, 0.0, 0.5)


def widths_by_tap(widths, straight, turned, wide):
    rows = wide.shape[1]
    total = widths.shape[1]
    first = pl.multiple_of(lax.axis_index("lat") * rows, 8)
    source = lax.broadcasted_iota(jnp.int32, (SPAN, TAPS), 0)
    tap_row = lax.broadcasted_iota(jnp.int32, (SPAN, TAPS), 1) // REACH
    values = widths[...].astype(jnp.float32).astype(jnp.bfloat16)
    for pick, table in ((source == tap_row, straight), (source == SPAN - 1 - tap_row, turned)):
        table[:8] = jnp.zeros((8, TAPS), jnp.float32)
        table[total + 8 :] = jnp.zeros((8, TAPS), jnp.float32)
        table[8 : total + 8] = lax.dot_general(
            values,
            pick.astype(jnp.bfloat16),
            (((0,), (0,)), ((), ())),
            preferred_element_type=jnp.float32,
        )
    tap_row = lax.broadcasted_iota(jnp.int32, (rows, TAPS), 1) // REACH
    read = first + lax.broadcasted_iota(jnp.int32, (rows, TAPS), 0) + tap_row - RAD
    on_grid = (read >= 0) & (read < total)
    wide[0] = jnp.where(on_grid, straight[pl.ds(first + 8, rows), :], -2.0)
    near = turned[pl.ds(first, rows + 16), :]
    value = near[8 - RAD : 8 - RAD + rows]
    for r in range(1, SPAN):
        value = jnp.where(tap_row == r, near[8 - RAD + r : 8 - RAD + r + rows], value)
    wide[1] = jnp.where(on_grid, value, -2.0)


def taps(foot_width):
    lane = lax.broadcasted_iota(jnp.int32, (BLOCK, TAPS), 1)
    tap_row = lane // REACH
    offset = (
        lane - tap_row * REACH - lax.broadcasted_iota(jnp.int32, (BLOCK, TAPS), 0) - HALO
    ).astype(jnp.float32)
    across = (tap_row[:1].astype(jnp.float32) - RAD) / (RAD + 1.0)
    norm = 3.0 / (2.0 * foot_width + 1.0)
    inside = jnp.abs(offset) <= foot_width
    along = offset * (1.0 / (foot_width + 1.0))
    pieces = []
    scales = [norm * jnp.maximum(0.0, 1.0 - 2.0 * jnp.abs(across - c)) for c in CENTERS]
    for lon_center in CENTERS:
        hat = jnp.maximum(0.0, 1.0 - 2.0 * jnp.abs(along - lon_center))
        hat = jnp.where(inside, hat, 0.0)
        pieces += [(hat * scale).astype(jnp.bfloat16) for scale in scales]
    return jnp.concatenate(pieces, axis=0)


def kernel(
    fields,
    cotangent,
    mixing,
    widths,
    features,
    gradient,
    cells,
    mixing_here,
    widths_here,
    straight,
    turned,
    wide,
    coeffs,
    basis,
    weights,
    load_sem,
    send_sem,
    recv_sem,
):
    rows, columns, channels = features.shape
    count = mixing.shape[0]
    inputs = (fields, cotangent)
    results = (features, gradient)
    here_lon, here_lat = lax.axis_index("lon"), lax.axis_index("lat")
    lons, lats = lax.axis_size("lon"), lax.axis_size("lat")
    east, west = lax.rem(here_lon + 1, lons), lax.rem(here_lon + lons - 1, lons)
    south, north = lax.rem(here_lat + 1, lats), lax.rem(here_lat + lats - 1, lats)

    barrier = pltpu.get_barrier_semaphore()
    for lat in (north, here_lat, south):
        for lon in (west, here_lon, east):
            if lat is here_lat and lon is here_lon:
                continue
            pl.semaphore_signal(
                barrier, inc=1, device_id=(lon, lat), device_id_type=pl.DeviceIdType.MESH
            )
    loads = []
    for side in range(2):
        load = pltpu.make_async_copy(
            inputs[side],
            cells.at[side, pl.ds(RAD, rows), pl.ds(HALO, columns)],
            load_sem.at[side],
        )
        load.start()
        loads.append(load)
    mix_load = pltpu.make_async_copy(mixing, mixing_here, load_sem.at[2])
    mix_load.start()
    width_load = pltpu.make_async_copy(widths, widths_here, load_sem.at[3])
    width_load.start()
    pl.semaphore_wait(barrier, 8)

    row_parts = (
        (north, 0, RAD, rows + RAD),
        (here_lat, 0, rows, RAD),
        (south, rows - RAD, RAD, 0),
    )
    column_parts = (
        (west, 0, HALO, columns + HALO),
        (here_lon, 0, columns, HALO),
        (east, columns - HALO, HALO, 0),
    )
    copies = {}
    for side in range(2):
        for place in ((0, 1), (2, 1), (1, 0), (1, 2), (0, 0), (0, 2), (2, 0), (2, 2)):
            lat, row_from, row_count, row_to = row_parts[place[0]]
            lon, column_from, column_count, column_to = column_parts[place[1]]
            slot = place[0] * 3 + place[1]
            copies[side, place] = pltpu.make_async_remote_copy(
                src_ref=inputs[side].at[pl.ds(row_from, row_count), pl.ds(column_from, column_count)],
                dst_ref=cells.at[side, pl.ds(row_to, row_count), pl.ds(column_to, column_count)],
                send_sem=send_sem.at[side, slot],
                recv_sem=recv_sem.at[side, slot],
                device_id=(lon, lat),
                device_id_type=pl.DeviceIdType.MESH,
            )
            copies[side, place].start()

    width_load.wait()
    widths_by_tap(widths_here, straight, turned, wide)
    mix_load.wait()
    for k in range(count):
        weights[0, k * channels : (k + 1) * channels, :] = mixing_here[k]
        weights[1, k * channels : (k + 1) * channels, :] = (
            mixing_here[count - 1 - k].astype(jnp.float32).T.astype(jnp.bfloat16)
        )

    def convolve(side, rows_here, parts, fresh):
        start, number, stride = rows_here

        def one_row(turn, carry):
            row = start + turn * stride
            if fresh:
                band = taps(wide[side, pl.ds(row, 1), :])
                coeffs[side, row] = band
            else:
                band = coeffs[side, row]
            data = jnp.concatenate(
                [
                    jnp.concatenate(
                        [
                            cells[side, row + r, BLOCK * b : BLOCK * b + REACH, :]
                            for r in range(SPAN)
                        ]
                        + [
                            cells[
                                side, row, BLOCK * b : BLOCK * b + TAPS - SPAN * REACH, :
                            ]
                        ],
                        axis=0,
                    )
                    for b in parts
                ],
                axis=1,
            )
            out = jnp.dot(band, data, preferred_element_type=jnp.float32).astype(jnp.bfloat16)
            for n in range(len(parts)):
                spot = (row * len(parts) + n) * BLOCK
                for k in range(count):
                    basis[side, pl.ds(spot, BLOCK), k * channels : (k + 1) * channels] = out[
                        k * BLOCK : (k + 1) * BLOCK, n * channels : (n + 1) * channels
                    ]
            return carry

        lax.fori_loop(0, number, one_row, 0, unroll=True)

    def mix(side, parts):
        size = rows * len(parts) * BLOCK
        mixed = jnp.dot(basis[side, :size, :], weights[side], preferred_element_type=jnp.float32)
        mixed = mixed.astype(jnp.bfloat16).reshape(rows, len(parts), BLOCK, channels)
        for n, b in enumerate(parts):
            results[side][:, BLOCK * b : BLOCK * (b + 1), :] = mixed[:, n]

    middle, rim = (1,), (0, 2)
    for side in range(2):
        loads[side].wait()
        convolve(side, (RAD, rows - 2 * RAD, 1), middle, True)
    for side in range(2):
        for place in ((0, 1), (2, 1)):
            copies[side, place].wait_recv()
    for side in range(2):
        convolve(side, (0, RAD, 1), middle, True)
        convolve(side, (rows - RAD, RAD, 1), middle, True)
    for side in range(2):
        mix(side, middle)
    for side in range(2):
        for place in ((1, 0), (1, 2), (0, 0), (0, 2), (2, 0), (2, 2)):
            copies[side, place].wait_recv()
        convolve(side, (0, rows, 1), rim, False)
        mix(side, rim)
    for copy in copies.values():
        copy.wait_send()


def body(fields, cotangent, mixing, widths):
    rows, columns, channels = fields.shape
    count = mixing.shape[0]
    shape = pltpu.VMEM(fields.shape, jnp.bfloat16)
    operands = [
        pltpu.with_memory_space_constraint(a, pltpu.HBM)
        for a in (fields, cotangent, mixing, widths.T)
    ]
    vmem = pl.BlockSpec(memory_space=pltpu.VMEM)
    hbm = pl.BlockSpec(memory_space=pltpu.HBM)
    return pl.pallas_call(
        kernel,
        out_shape=(shape, shape),
        in_specs=[hbm, hbm, hbm, hbm],
        out_specs=(vmem, vmem),
        scratch_shapes=[
            pltpu.VMEM((2, rows + 2 * RAD, columns + 2 * HALO, channels), jnp.bfloat16),
            pltpu.VMEM(mixing.shape, jnp.bfloat16),
            pltpu.VMEM((SPAN, widths.shape[0]), jnp.int32),
            pltpu.VMEM((widths.shape[0] + 16, TAPS), jnp.float32),
            pltpu.VMEM((widths.shape[0] + 16, TAPS), jnp.float32),
            pltpu.VMEM((2, rows, TAPS), jnp.float32),
            pltpu.VMEM((2, rows, count * BLOCK, TAPS), jnp.bfloat16),
            pltpu.VMEM((2, rows * 2 * BLOCK, count * channels), jnp.bfloat16),
            pltpu.VMEM((2, count * channels, channels), jnp.bfloat16),
            pltpu.SemaphoreType.DMA((4,)),
            pltpu.SemaphoreType.DMA((2, 9)),
            pltpu.SemaphoreType.DMA((2, 9)),
        ],
        compiler_params=pltpu.CompilerParams(
            collective_id=0, has_side_effects=True, vmem_limit_bytes=40 * 1024 * 1024
        ),
    )(*operands)


def solution(mesh):
    in_specs = (P("lat", "lon", None), P("lat", "lon", None), P(), P())
    out_specs = (P("lat", "lon", None), P("lat", "lon", None))
    return jax.shard_map(body, mesh=mesh, in_specs=in_specs, out_specs=out_specs, check_vma=False)
```

time: 66.3 us -> 32.8 us (0.49); the launches traced: 65.1 us -> 32.5 us
  starting transfers between devices: 20.2 us -> 0 us
  waiting for transfers between devices: 15.1 us -> 0 us
  Pallas kernels: 25.5 us -> 30.2 us
  other arithmetic: 3.44 us -> 0 us
  local copies, waits for them, and re-layouts: 0.21 us -> 1.63 us
    ppermute x4 -> x0, starting transfers between devices: 20.2 us -> none  [the longest x2 17 us: padded_2(): lax.ppermute(tail, axis, [(i, (i + 1) % count) for i in range(ends)])]
    ppermute x4 -> x0, waiting for transfers between devices: 15.1 us -> none  [the longest x2 12.2 us: padded_2(): lax.ppermute(head, axis, [((i + 1) % count, i) for i in range(ends)])]
    pallas_call x1, Pallas kernels: 25.5 us -> 30.2 us  [body(): pl.pallas_call(kernel, out_shape=(shape, shape), in_specs=[hbm, hbm, hbm,...]
    slice x2 -> x0, other arithmetic: 2.28 us -> none  [padded_2(): lax.slice_in_dim(cells, cells.shape[dim] - width, cells.shape[dim], axis=...]
    unnamed x9 -> x2, local copies, waits for them, and re-layouts: 0.21 us -> 1.63 us
    concatenate x1 -> x0, other arithmetic: 1.17 us -> none  [padded_2(): jnp.concatenate([lax.ppermute(tail, axis, [(i, (i + 1) % count) for i in...]
  transfers between devices with their start and end apart: 4 -> 0, of which waited for: 3 -> 0; matrix products, arithmetic and copies ran while one was open for 0% -> 0% of each run, Pallas kernels for 0% -> 0%
where the time goes in v1:
time: 32.8 us; the launch traced here: 32.5 us
  Pallas kernels  30.2 us (92%)
  local copies, waits for them, and re-layouts  1.63 us (5%)
  between operations  0.64 us (2%)
    pallas_call x1, Pallas kernels, body(): pl.pallas_call(kernel, out_shape=(shape, shape), in_specs=[hbm, hbm, hbm,...  30.2 us
    unnamed x2, local copies, waits for them, and re-layouts  1.63 us

profile of v1, /device:TPU:1, one launch (start us, length us, event | category | flops | bytes accessed | tf_op | source)
XLA Modules:
  0.0 32.5 jit_solution(11464599651161248883)
XLA Ops:
  0.6 30.2 %shard_map.59 = (bf16[48,48,128]{2,1,0:T(8,128)(2,1)S(1)}, bf16[48,48,128]{2,1,0:T(8,128)(2,1)S(1)}) custom-call(bf16[48,48,128]{2,1,0:T(8,128)(2,1)} %fields.1, bf16[48,48,128]{2,1,0:T(8,128)(2,1)} %cotangent.1, bf16[9,128,128]{2,1,0:T(8,128)(2,1)} %mixing.1, s32[5,768]{1,0:T(8,128)} %bitcast.1), custom_call_target="tpu_custom_call" | custom-call | tf_op jit(solution)/shard_map/pallas_call | solution.py:229
  30.8 0.8 %copy.8 = bf16[48,48,128]{2,1,0:T(8,128)(2,1)} copy(bf16[48,48,128]{2,1,0:T(8,128)(2,1)S(1)} %get-tuple-element.2) | data formatting | bytes 1179648
  31.7 0.8 %copy.9 = bf16[48,48,128]{2,1,0:T(8,128)(2,1)} copy(bf16[48,48,128]{2,1,0:T(8,128)(2,1)S(1)} %get-tuple-element.3) | data formatting | bytes 1179648

commit v2 on v1

v2 whole, which is shorter than its diff:
```python
import functools

import jax
import jax.numpy as jnp
from jax import lax
from jax.experimental import pallas as pl
from jax.experimental.pallas import tpu as pltpu
from jax.sharding import PartitionSpec as P

RAD = 2
HALO = 16
SPAN = 2 * RAD + 1
BLOCK = 16
REACH = BLOCK + 2 * HALO
TAPS = 256
CENTERS = (-0.5, 0.0, 0.5)


def widths_by_tap(widths, straight, turned, wide):
    rows = wide.shape[1]
    total = widths.shape[1]
    first = pl.multiple_of(lax.axis_index("lat") * rows, 8)
    source = lax.broadcasted_iota(jnp.int32, (SPAN, TAPS), 0)
    tap_row = lax.broadcasted_iota(jnp.int32, (SPAN, TAPS), 1) // REACH
    values = widths[...].astype(jnp.float32).astype(jnp.bfloat16)
    for pick, table in ((source == tap_row, straight), (source == SPAN - 1 - tap_row, turned)):
        table[:8] = jnp.zeros((8, TAPS), jnp.float32)
        table[total + 8 :] = jnp.zeros((8, TAPS), jnp.float32)
        table[8 : total + 8] = lax.dot_general(
            values,
            pick.astype(jnp.bfloat16),
            (((0,), (0,)), ((), ())),
            preferred_element_type=jnp.float32,
        )
    tap_row = lax.broadcasted_iota(jnp.int32, (rows, TAPS), 1) // REACH
    read = first + lax.broadcasted_iota(jnp.int32, (rows, TAPS), 0) + tap_row - RAD
    on_grid = (read >= 0) & (read < total)
    wide[0] = jnp.where(on_grid, straight[pl.ds(first + 8, rows), :], -2.0)
    near = turned[pl.ds(first, rows + 16), :]
    value = near[8 - RAD : 8 - RAD + rows]
    for r in range(1, SPAN):
        value = jnp.where(tap_row == r, near[8 - RAD + r : 8 - RAD + r + rows], value)
    wide[1] = jnp.where(on_grid, value, -2.0)


def taps(foot_width):
    lane = lax.broadcasted_iota(jnp.int32, (BLOCK, TAPS), 1)
    tap_row = lane // REACH
    offset = (
        lane - tap_row * REACH - lax.broadcasted_iota(jnp.int32, (BLOCK, TAPS), 0) - HALO
    ).astype(jnp.float32)
    across = (tap_row[:1].astype(jnp.float32) - RAD) / (RAD + 1.0)
    norm = 3.0 / (2.0 * foot_width + 1.0)
    inside = jnp.abs(offset) <= foot_width
    along = offset * (1.0 / (foot_width + 1.0))
    pieces = []
    scales = [norm * jnp.maximum(0.0, 1.0 - 2.0 * jnp.abs(across - c)) for c in CENTERS]
    for lon_center in CENTERS:
        hat = jnp.maximum(0.0, 1.0 - 2.0 * jnp.abs(along - lon_center))
        hat = jnp.where(inside, hat, 0.0)
        pieces += [(hat * scale).astype(jnp.bfloat16) for scale in scales]
    return jnp.concatenate(pieces, axis=0)


def kernel(
    fields,
    cotangent,
    mixing,
    widths,
    features,
    gradient,
    cells,
    mixing_here,
    widths_here,
    straight,
    turned,
    wide,
    coeffs,
    basis,
    edge_basis,
    weights,
    load_sem,
    send_sem,
    recv_sem,
    lon_in,
    lat_in,
):
    rows, columns, channels = features.shape
    count = mixing.shape[0]
    inputs = (fields, cotangent)
    results = (features, gradient)
    here_lon, here_lat = lax.axis_index("lon"), lax.axis_index("lat")
    lons, lats = lax.axis_size("lon"), lax.axis_size("lat")
    east, west = lax.rem(here_lon + 1, lons), lax.rem(here_lon + lons - 1, lons)
    south, north = lax.rem(here_lat + 1, lats), lax.rem(here_lat + lats - 1, lats)
    odd = lax.rem(here_lon, 2)
    lead = here_lon - odd
    barrier = pltpu.get_barrier_semaphore()

    def tell(sem, lon, lat):
        pl.semaphore_signal(sem, inc=1, device_id=(lon, lat), device_id_type=pl.DeviceIdType.MESH)

    @pl.when(odd == 0)
    def _():
        tell(barrier, lax.rem(here_lon + lons - 2, lons), here_lat)

    @pl.when(odd == 1)
    def _():
        tell(barrier, lead, here_lat)
        tell(barrier, east, here_lat)

    beside = lax.rem(here_lon + lons - 1 + 3 * odd, lons)
    for lat in (north, south):
        tell(barrier, lead + 1, lat)
        tell(barrier, beside, lat)

    loads = []
    for side in range(2):
        loads.append(
            pltpu.make_async_copy(
                inputs[side],
                cells.at[side, pl.ds(RAD, rows), pl.ds(HALO, columns)],
                load_sem.at[side],
            )
        )
    mix_load = pltpu.make_async_copy(mixing, mixing_here, load_sem.at[2])
    width_load = pltpu.make_async_copy(widths, widths_here, load_sem.at[3])
    for load in (*loads, width_load, mix_load):
        load.start()

    def remote(source, target, sems, lon, lat):
        return pltpu.make_async_remote_copy(
            src_ref=source,
            dst_ref=target,
            send_sem=sems[0].at[sems[1]],
            recv_sem=sems[2].at[sems[1]],
            device_id=(lon, lat),
            device_id_type=pl.DeviceIdType.MESH,
        )

    near_copies, far_copies, lat_copies = [], [], []
    last = columns + HALO
    mate = here_lon + 1 - 2 * odd
    away = lax.rem(here_lon + lons - 1 + 2 * odd, lons)
    low, high = pl.multiple_of(odd * last, HALO), pl.multiple_of((1 - odd) * last, HALO)
    near_take = pl.multiple_of((1 - odd) * (columns - HALO), HALO)
    far_take = pl.multiple_of(odd * (columns - HALO), HALO)
    for side in range(2):
        for slot, (copies, lon, take, give) in enumerate(
            ((near_copies, mate, near_take, low), (far_copies, away, far_take, high))
        ):
            copies.append(
                remote(
                    inputs[side].at[:, pl.ds(take, HALO)],
                    cells.at[side, pl.ds(RAD, rows), pl.ds(give, HALO)],
                    (send_sem, 2 * side + slot, recv_sem),
                    lon,
                    here_lat,
                )
            )
    for way, (lat, take, give) in enumerate(((north, RAD, rows + RAD), (south, rows, 0))):
        lat_copies.append(
            remote(
                cells.at[:, pl.ds(take, RAD), pl.ds(HALO, columns)],
                cells.at[:, pl.ds(give, RAD), pl.ds(HALO, columns)],
                (send_sem, 4 + way, recv_sem),
                here_lon,
                lat,
            )
        )
    corners = (
        (north, RAD, rows + RAD, west, HALO, last),
        (north, RAD, rows + RAD, east, columns, 0),
        (south, rows, 0, west, HALO, last),
        (south, rows, 0, east, columns, 0),
    )
    for slot, (lat, row_take, row_give, lon, take, give) in enumerate(corners):
        lat_copies.append(
            remote(
                cells.at[:, pl.ds(row_take, RAD), pl.ds(take, HALO)],
                cells.at[:, pl.ds(row_give, RAD), pl.ds(give, HALO)],
                (send_sem, 6 + slot, recv_sem),
                lon,
                lat,
            )
        )

    @pl.when(odd == 0)
    def _():
        pl.semaphore_wait(barrier, 3)
        tell(lon_in, lead + 1, here_lat)

    @pl.when(odd == 1)
    def _():
        pl.semaphore_wait(lon_in, 1)

    def send_lat():
        @pl.when(odd == 1)
        def _():
            pl.semaphore_wait(barrier, 8)
            tell(lat_in, lead, here_lat)

        @pl.when(odd == 0)
        def _():
            pl.semaphore_wait(lat_in, 1)

        for copy in lat_copies:
            copy.start()

    for copy in near_copies:
        copy.start()
    for load in loads:
        load.wait()

    @pl.when(lax.rem(here_lat, 2) == 1)
    def _():
        send_lat()

    for copy in far_copies:
        copy.start()

    width_load.wait()
    widths_by_tap(widths_here, straight, turned, wide)
    mix_load.wait()
    for k in range(count):
        weights[0, k * channels : (k + 1) * channels, :] = mixing_here[k]
        weights[1, k * channels : (k + 1) * channels, :] = (
            mixing_here[count - 1 - k].astype(jnp.float32).T.astype(jnp.bfloat16)
        )

    def convolve(side, row, spot, target, parts, fresh):
        if fresh:
            band = taps(wide[side, pl.ds(row, 1), :])
            coeffs[side, row] = band
        else:
            band = coeffs[side, row]
        data = jnp.concatenate(
            [
                jnp.concatenate(
                    [cells[side, row + r, pl.ds(b, REACH), :] for r in range(SPAN)]
                    + [cells[side, row, pl.ds(b, TAPS - SPAN * REACH), :]],
                    axis=0,
                )
                for b in parts
            ],
            axis=1,
        )
        out = jnp.dot(band, data, preferred_element_type=jnp.float32).astype(jnp.bfloat16)
        for n in range(len(parts)):
            for k in range(count):
                target[
                    side, pl.ds(spot + n * BLOCK, BLOCK), k * channels : (k + 1) * channels
                ] = out[k * BLOCK : (k + 1) * BLOCK, n * channels : (n + 1) * channels]

    def convolve_inner(side, parts, fresh):
        def one_row(row, carry):
            spot = (row - RAD) * len(parts) * BLOCK
            convolve(side, row, spot, basis, parts, fresh)
            return carry

        lax.fori_loop(RAD, rows - RAD, one_row, 0, unroll=True)

    def mix_inner(side, parts):
        size = (rows - 2 * RAD) * len(parts) * BLOCK
        mixed = jnp.dot(basis[side, :size, :], weights[side], preferred_element_type=jnp.float32)
        mixed = mixed.astype(jnp.bfloat16).reshape(-1, len(parts), BLOCK, channels)
        for n, b in enumerate(parts):
            results[side][RAD : rows - RAD, pl.ds(b, BLOCK), :] = mixed[:, n]

    near = pl.multiple_of((1 - odd) * (columns - BLOCK), BLOCK)
    far = pl.multiple_of(odd * (columns - BLOCK), BLOCK)
    for side in range(2):
        near_copies[side].wait_recv()
        convolve_inner(side, (BLOCK, near), True)
    for side in range(2):
        mix_inner(side, (BLOCK, near))

    @pl.when(lax.rem(here_lat, 2) == 0)
    def _():
        send_lat()

    for side in range(2):
        far_copies[side].wait_recv()
        convolve_inner(side, (far,), False)
        mix_inner(side, (far,))

    for copy in lat_copies:
        copy.wait_recv()
    outer = (*range(RAD), *range(rows - RAD, rows))
    whole = (0, BLOCK, 2 * BLOCK)
    for side in range(2):
        for e, row in enumerate(outer):
            convolve(side, row, e * columns, edge_basis, whole, True)
    for side in range(2):
        mixed = jnp.dot(edge_basis[side], weights[side], preferred_element_type=jnp.float32)
        mixed = mixed.astype(jnp.bfloat16).reshape(len(outer), columns, channels)
        for e, row in enumerate(outer):
            results[side][row] = mixed[e]
    for copy in (*near_copies, *far_copies, *lat_copies):
        copy.wait_send()


def body(fields, cotangent, mixing, widths):
    rows, columns, channels = fields.shape
    count = mixing.shape[0]
    shape = pltpu.VMEM(fields.shape, jnp.bfloat16)
    operands = [
        pltpu.with_memory_space_constraint(a, pltpu.HBM)
        for a in (fields, cotangent, mixing, widths.T)
    ]
    vmem = pl.BlockSpec(memory_space=pltpu.VMEM)
    hbm = pl.BlockSpec(memory_space=pltpu.HBM)
    return pl.pallas_call(
        kernel,
        out_shape=(shape, shape),
        in_specs=[hbm, hbm, hbm, hbm],
        out_specs=(vmem, vmem),
        scratch_shapes=[
            pltpu.VMEM((2, rows + 2 * RAD, columns + 2 * HALO, channels), jnp.bfloat16),
            pltpu.VMEM(mixing.shape, jnp.bfloat16),
            pltpu.VMEM((SPAN, widths.shape[0]), jnp.int32),
            pltpu.VMEM((widths.shape[0] + 16, TAPS), jnp.float32),
            pltpu.VMEM((widths.shape[0] + 16, TAPS), jnp.float32),
            pltpu.VMEM((2, rows, TAPS), jnp.float32),
            pltpu.VMEM((2, rows, count * BLOCK, TAPS), jnp.bfloat16),
            pltpu.VMEM((2, rows * 2 * BLOCK, count * channels), jnp.bfloat16),
            pltpu.VMEM((2, 2 * RAD * columns, count * channels), jnp.bfloat16),
            pltpu.VMEM((2, count * channels, channels), jnp.bfloat16),
            pltpu.SemaphoreType.DMA((4,)),
            pltpu.SemaphoreType.DMA((10,)),
            pltpu.SemaphoreType.DMA((10,)),
            pltpu.SemaphoreType.REGULAR,
            pltpu.SemaphoreType.REGULAR,
        ],
        compiler_params=pltpu.CompilerParams(
            collective_id=0, has_side_effects=True, vmem_limit_bytes=40 * 1024 * 1024
        ),
    )(*operands)


def solution(mesh):
    in_specs = (P("lat", "lon", None), P("lat", "lon", None), P(), P())
    out_specs = (P("lat", "lon", None), P("lat", "lon", None))
    return jax.shard_map(body, mesh=mesh, in_specs=in_specs, out_specs=out_specs, check_vma=False)
```

time: 32.8 us -> 26.9 us (0.82)
  Pallas kernels: 30.2 us -> 24.4 us
    pallas_call x1, Pallas kernels: 30.2 us -> 24.4 us  [body(): pl.pallas_call(kernel, out_shape=(shape, shape), in_specs=[hbm, hbm, hbm,...]
where the time goes in v2:
time: 26.9 us; the launch traced here: 26.6 us
  Pallas kernels  24.4 us (91%)
  local copies, waits for them, and re-layouts  1.63 us (6%)
  between operations  0.64 us (2%)
    pallas_call x1, Pallas kernels, body(): pl.pallas_call(kernel, out_shape=(shape, shape), in_specs=[hbm, hbm, hbm,...  24.4 us
    unnamed x2, local copies, waits for them, and re-layouts  1.63 us

profile of v2, /device:TPU:1, one launch (start us, length us, event | category | flops | bytes accessed | tf_op | source)
XLA Modules:
  0.0 26.6 jit_solution(12143568919217198703)
XLA Ops:
  0.6 24.4 %shard_map.59 = (bf16[48,48,128]{2,1,0:T(8,128)(2,1)S(1)}, bf16[48,48,128]{2,1,0:T(8,128)(2,1)S(1)}) custom-call(bf16[48,48,128]{2,1,0:T(8,128)(2,1)} %fields.1, bf16[48,48,128]{2,1,0:T(8,128)(2,1)} %cotangent.1, bf16[9,128,128]{2,1,0:T(8,128)(2,1)} %mixing.1, s32[5,768]{1,0:T(8,128)} %bitcast.1), custom_call_target="tpu_custom_call" | custom-call | tf_op jit(solution)/shard_map/pallas_call | solution.py:313
  25.0 0.8 %copy.8 = bf16[48,48,128]{2,1,0:T(8,128)(2,1)} copy(bf16[48,48,128]{2,1,0:T(8,128)(2,1)S(1)} %get-tuple-element.2) | data formatting | bytes 1179648
  25.8 0.8 %copy.9 = bf16[48,48,128]{2,1,0:T(8,128)(2,1)} copy(bf16[48,48,128]{2,1,0:T(8,128)(2,1)S(1)} %get-tuple-element.3) | data formatting | bytes 1179648

commit v3 on v2

--- a/solution.py
+++ b/solution.py
@@ -13,6 +13,7 @@
 BLOCK = 16
 REACH = BLOCK + 2 * HALO
 TAPS = 256
+RUN = 8
 CENTERS = (-0.5, 0.0, 0.5)
 
 
@@ -279,25 +280,68 @@
     def _():
         send_lat()
 
-    for side in range(2):
-        far_copies[side].wait_recv()
-        convolve_inner(side, (far,), False)
-        mix_inner(side, (far,))
-
-    for copy in lat_copies:
-        copy.wait_recv()
-    outer = (*range(RAD), *range(rows - RAD, rows))
-    whole = (0, BLOCK, 2 * BLOCK)
-    for side in range(2):
-        for e, row in enumerate(outer):
-            convolve(side, row, e * columns, edge_basis, whole, True)
-    for side in range(2):
-        mixed = jnp.dot(edge_basis[side], weights[side], preferred_element_type=jnp.float32)
-        mixed = mixed.astype(jnp.bfloat16).reshape(len(outer), columns, channels)
-        for e, row in enumerate(outer):
-            results[side][row] = mixed[e]
+    def far_rows(side, first, number):
+        def one_row(row, carry):
+            convolve(side, row, (row - first) * BLOCK, basis, (far,), False)
+            return carry
+
+        lax.fori_loop(first, first + number, one_row, 0, unroll=True)
+        mixed = jnp.dot(
+            basis[side, : number * BLOCK, :], weights[side], preferred_element_type=jnp.float32
+        )
+        results[side][first : first + number, pl.ds(far, BLOCK), :] = (
+            mixed.astype(jnp.bfloat16).reshape(number, BLOCK, channels)
+        )
+
+    def edge_rows(parts):
+        outer = (*range(RAD), *range(rows - RAD, rows))
+        for side in range(2):
+            for e, row in enumerate(outer):
+                convolve(side, row, e * len(parts) * BLOCK, edge_basis, parts, True)
+        size = len(outer) * len(parts) * BLOCK
+        for side in range(2):
+            mixed = jnp.dot(
+                edge_basis[side, :size, :], weights[side], preferred_element_type=jnp.float32
+            )
+            mixed = mixed.astype(jnp.bfloat16).reshape(len(outer), len(parts), BLOCK, channels)
+            for e, row in enumerate(outer):
+                for n, b in enumerate(parts):
+                    results[side][row, pl.ds(b, BLOCK), :] = mixed[e, n]
+
+    place = lax.rem(here_lon + 1, RUN)
+    far_last = (lax.rem(here_lat, 2) == 1) & (place <= 1)
+
+    @pl.when(far_last)
+    def _():
+        for copy in lat_copies:
+            copy.wait_recv()
+        edge_rows((BLOCK, near))
+        for side in range(2):
+            far_copies[side].wait_recv()
+            far_rows(side, 0, rows)
+
+    @pl.when(jnp.logical_not(far_last))
+    def _():
+        for side in range(2):
+            far_copies[side].wait_recv()
+            far_rows(side, RAD, rows - 2 * RAD)
+        for copy in lat_copies:
+            copy.wait_recv()
+        edge_rows((0, BLOCK, 2 * BLOCK))
+
     for copy in (*near_copies, *far_copies, *lat_copies):
         copy.wait_send()
+
+
+def deliver(features, gradient, features_out, gradient_out, sem):
+    copies = [
+        pltpu.make_async_copy(features, features_out, sem.at[0]),
+        pltpu.make_async_copy(gradient, gradient_out, sem.at[1]),
+    ]
+    for copy in copies:
+        copy.start()
+    for copy in copies:
+        copy.wait()
 
 
 def body(fields, cotangent, mixing, widths):
@@ -310,7 +354,7 @@
     ]
     vmem = pl.BlockSpec(memory_space=pltpu.VMEM)
     hbm = pl.BlockSpec(memory_space=pltpu.HBM)
-    return pl.pallas_call(
+    results = pl.pallas_call(
         kernel,
         out_shape=(shape, shape),
         in_specs=[hbm, hbm, hbm, hbm],
@@ -336,6 +380,16 @@
             collective_id=0, has_side_effects=True, vmem_limit_bytes=40 * 1024 * 1024
         ),
     )(*operands)
+    results = [pltpu.with_memory_space_constraint(a, pltpu.VMEM) for a in results]
+    anywhere = pl.BlockSpec(memory_space=pl.ANY)
+    final = jax.ShapeDtypeStruct(fields.shape, jnp.bfloat16)
+    return pl.pallas_call(
+        deliver,
+        out_shape=(final, final),
+        in_specs=[vmem, vmem],
+        out_specs=(anywhere, anywhere),
+        scratch_shapes=[pltpu.SemaphoreType.DMA((2,))],
+    )(*results)
 
 
 def solution(mesh):

time: 26.9 us -> 26.3 us (0.978)
  local copies, waits for them, and re-layouts: 1.63 us -> 0 us
  Pallas kernels: 24.4 us -> 25.4 us
    unnamed x2 -> x0, local copies, waits for them, and re-layouts: 1.63 us -> none
    pallas_call x0 -> x1, Pallas kernels: none -> 1.03 us  [body(): pl.pallas_call(deliver, out_shape=(final, final), in_specs=[vmem, vmem],...]
where the time goes in v3:
time: 26.3 us; the launch traced here: 26.2 us
  Pallas kernels  25.4 us (97%)
  between operations  0.8 us (3%)
    pallas_call x1, Pallas kernels, body(): pl.pallas_call(kernel, out_shape=(shape, shape), in_specs=[hbm, hbm, hbm,...  24.4 us
    pallas_call x1, Pallas kernels, body(): pl.pallas_call(deliver, out_shape=(final, final), in_specs=[vmem, vmem],...  1.03 us

profile of v3, /device:TPU:1, one launch (start us, length us, event | category | flops | bytes accessed | tf_op | source)
XLA Modules:
  0.0 26.2 jit_solution(15538583178159072516)
XLA Ops:
  0.6 24.4 %shard_map.59 = (bf16[48,48,128]{2,1,0:T(8,128)(2,1)S(1)}, bf16[48,48,128]{2,1,0:T(8,128)(2,1)S(1)}) custom-call(bf16[48,48,128]{2,1,0:T(8,128)(2,1)} %fields.1, bf16[48,48,128]{2,1,0:T(8,128)(2,1)} %cotangent.1, bf16[9,128,128]{2,1,0:T(8,128)(2,1)} %mixing.1, s32[5,768]{1,0:T(8,128)} %bitcast.1), custom_call_target="tpu_custom_call" | custom-call | tf_op jit(solution)/shard_map/pallas_call | solution.py:357
  25.0 1.0 %shard_map.60 = (bf16[48,48,128]{2,1,0:T(8,128)(2,1)}, bf16[48,48,128]{2,1,0:T(8,128)(2,1)}) custom-call(bf16[48,48,128]{2,1,0:T(8,128)(2,1)S(1)} %get-tuple-element.4.features, bf16[48,48,128]{2,1,0:T(8,128)(2,1)S(1)} %get-tuple-element.5.gradient), custom_call_target="tpu_custom_call" | custom-call | tf_op jit(solution)/shard_map/pallas_call | solution.py:386

commit v4 on v3

--- a/solution.py
+++ b/solution.py
@@ -276,6 +276,10 @@
     for side in range(2):
         mix_inner(side, (BLOCK, near))
 
+    for side in range(2):
+        for row in (*range(RAD), *range(rows - RAD, rows)):
+            coeffs[side, row] = taps(wide[side, pl.ds(row, 1), :])
+
     @pl.when(lax.rem(here_lat, 2) == 0)
     def _():
         send_lat()
@@ -297,7 +301,7 @@
         outer = (*range(RAD), *range(rows - RAD, rows))
         for side in range(2):
             for e, row in enumerate(outer):
-                convolve(side, row, e * len(parts) * BLOCK, edge_basis, parts, True)
+                convolve(side, row, e * len(parts) * BLOCK, edge_basis, parts, False)
         size = len(outer) * len(parts) * BLOCK
         for side in range(2):
             mixed = jnp.dot(

time: 26.3 us -> 26.3 us (level)
  no operation moved by 1% of the time
where the time goes in v4:
time: 26.3 us; the launch traced here: 26.2 us
  Pallas kernels  25.4 us (97%)
  between operations  0.8 us (3%)
    pallas_call x1, Pallas kernels, body(): pl.pallas_call(kernel, out_shape=(shape, shape), in_specs=[hbm, hbm, hbm,...  24.4 us
    pallas_call x1, Pallas kernels, body(): pl.pallas_call(deliver, out_shape=(final, final), in_specs=[vmem, vmem],...  1.03 us

profile of v4, /device:TPU:1, one launch (start us, length us, event | category | flops | bytes accessed | tf_op | source)
XLA Modules:
  0.0 26.2 jit_solution(14849226852665626759)
XLA Ops:
  0.6 24.4 %shard_map.59 = (bf16[48,48,128]{2,1,0:T(8,128)(2,1)S(1)}, bf16[48,48,128]{2,1,0:T(8,128)(2,1)S(1)}) custom-call(bf16[48,48,128]{2,1,0:T(8,128)(2,1)} %fields.1, bf16[48,48,128]{2,1,0:T(8,128)(2,1)} %cotangent.1, bf16[9,128,128]{2,1,0:T(8,128)(2,1)} %mixing.1, s32[5,768]{1,0:T(8,128)} %bitcast.1), custom_call_target="tpu_custom_call" | custom-call | tf_op jit(solution)/shard_map/pallas_call | solution.py:361
  25.0 1.0 %shard_map.60 = (bf16[48,48,128]{2,1,0:T(8,128)(2,1)}, bf16[48,48,128]{2,1,0:T(8,128)(2,1)}) custom-call(bf16[48,48,128]{2,1,0:T(8,128)(2,1)S(1)} %get-tuple-element.4.features, bf16[48,48,128]{2,1,0:T(8,128)(2,1)S(1)} %get-tuple-element.5.gradient), custom_call_target="tpu_custom_call" | custom-call | tf_op jit(solution)/shard_map/pallas_call | solution.py:390
